TPU v7x, 256 devices: a whole 4x4x8 slice. The times are simulated.
256 devices in a mesh: ctx: 32 (over y, z), head: 8 (over x, core).
Axes of the slice: x: 4, y: 4, z: 8, core: 2. Of those that a mesh axis runs over, the one named last changes fastest.
Arguments:
- queries: bfloat16 [16384, 4096], P('ctx', 'head'), may hold values from -48 to 48
- key_rows: bfloat16 [16384, 1024], P('ctx', 'head'), may hold values from -48 to 48
- value_rows: bfloat16 [16384, 1024], P('ctx', 'head'), may hold values from -6 to 6
- kept_positions: int32 [8, 8192], P('head', 'ctx'), may hold values from 0 to 511, as said below
- anchor_length: int32 [8], P('head'), may hold values from 128 to 512
- output_weight: bfloat16 [4096, 4096], P('head'), may hold values from -0.125 to 0.125
Outputs:
- layer_output: bfloat16 [16384, 4096], P('ctx', 'head')
Inputs may be any that keep to these rules, and one draw needn't show every extreme that they name: `kept_positions`: for each key-value head and block, 256 distinct positions of that block.
All inputs are finite; a program needn't handle non-finite values.
Results may differ from a plain program's by a relative error of at most 0.02.
Values may be sent and summed in bfloat16 or wider, within the bound.
No kernel may reach another device: no remote copies, remote signals or barrier semaphores. Data moves between devices by JAX's collectives and lax.ppermute only.
A program may use at most 192 MiB of HBM per device.

v0:
```python
import jax
import jax.numpy as jnp
from jax import lax
from jax.sharding import PartitionSpec as P

ANCHOR = 512


NEGATIVE = -1e30


def from_root(shard, axis, root):
    mine = lax.axis_index(axis) == root
    return lax.psum(jnp.where(mine, shard, jnp.zeros_like(shard)), axis)


def passed_along(block, axis, distance):
    devices = range(lax.axis_size(axis))
    route = [(i - distance, i) for i in devices if i - distance in devices]
    return lax.ppermute(block, axis, route)


def absorb(state, queries4, kept, vals, allowed, scale):
    peak, total, accum = state
    heads_kv = queries4.shape[1]
    width = kept.shape[0]
    key_three = kept.reshape(width, heads_kv, -1)
    val_three = vals.reshape(width, heads_kv, -1)
    scores = (
        jnp.einsum("qhgd,khd->hgqk", queries4, key_three, preferred_element_type=jnp.float32)
        * scale
    )
    scores = jnp.where(allowed, scores, NEGATIVE)
    new_peak = jnp.maximum(peak, jnp.max(scores, axis=-1))
    weights = jnp.where(allowed, jnp.exp(scores - new_peak[..., None]), 0.0)
    factor = jnp.exp(peak - new_peak)
    total = total * factor + jnp.sum(weights, axis=-1)
    accum = accum * factor[..., None] + jnp.einsum(
        "hgqk,khd->hgqd",
        weights.astype(jnp.bfloat16),
        val_three,
        preferred_element_type=jnp.float32,
    )
    return (new_peak, total, accum)


def on_device(queries, key_rows, value_rows, kept_positions, anchor_length, output_weight):
    length = queries.shape[0]
    heads_kv = kept_positions.shape[0]
    keep = kept_positions.shape[1]
    head_dim = key_rows.shape[1] // heads_kv
    group = queries.shape[1] // key_rows.shape[1]
    scale = head_dim ** (-0.5)
    mine = lax.axis_index("ctx")
    queries4 = queries.reshape(length, heads_kv, group, head_dim)
    key_three = key_rows.reshape(length, heads_kv, head_dim)
    val_three = value_rows.reshape(length, heads_kv, head_dim)
    selector = jnp.arange(heads_kv)[:, None]
    kept_keys = (
        key_three[kept_positions, selector].transpose(1, 0, 2).reshape(keep, heads_kv * head_dim)
    )
    kept_vals = (
        val_three[kept_positions, selector].transpose(1, 0, 2).reshape(keep, heads_kv * head_dim)
    )
    state = (
        jnp.full((heads_kv, group, length), NEGATIVE, jnp.float32),
        jnp.zeros((heads_kv, group, length), jnp.float32),
        jnp.zeros((heads_kv, group, length, head_dim), jnp.float32),
    )
    anchor_keys, anchor_vals = (from_root(key_rows, "ctx", 0), from_root(value_rows, "ctx", 0))
    anchor_ok = (jnp.arange(ANCHOR)[None, :] < anchor_length[:, None]) & (mine > 0)
    state = absorb(state, queries4, anchor_keys, anchor_vals, anchor_ok[:, None, None, :], scale)
    span = min(length, 512)
    positions = jnp.arange(length)[:, None]
    allowed = jnp.arange(span)[None, :] + 0 <= positions
    state = absorb(state, queries4, key_rows, value_rows, allowed, scale)

    def relay(step, carry):
        inner, moving = carry
        moving = passed_along(moving, "ctx", 1)
        allowed = jnp.broadcast_to(mine > step, (length, keep))
        inner = absorb(inner, queries4, moving[0], moving[1], allowed, scale)
        return (inner, moving)

    state, moving = lax.fori_loop(
        0, lax.axis_size("ctx") - 1, relay, (state, jnp.stack([kept_keys, kept_vals]))
    )
    peak, total, accum = state
    attention = (
        (accum / total[..., None]).transpose(2, 0, 1, 3).reshape(length, -1).astype(jnp.bfloat16)
    )
    partial_value = jnp.dot(attention, output_weight, preferred_element_type=jnp.float32)
    return lax.psum_scatter(
        partial_value.astype(jnp.bfloat16), "head", scatter_dimension=1, tiled=True
    )


def solution(mesh):
    placed = (
        P("ctx", "head"),
        P("ctx", "head"),
        P("ctx", "head"),
        P("head", "ctx"),
        P("head"),
        P("head", None),
    )
    return jax.shard_map(
        on_device, mesh=mesh, in_specs=placed, out_specs=P("ctx", "head"), check_vma=False
    )
```

profile of v0, /device:TPU:30, one launch (start us, length us, event | category | flops | bytes accessed | tf_op | source)
XLA Modules:
  0.0 562.1 jit_solution(3606734711832974172)
XLA Ops:
  17.6 138.7 %all-reduce.4.cloned.1.call-done = (bf16[512,128]{1,0:T(8,128)(2,1)}, bf16[512,128]{1,0:T(8,128)(2,1)}) async-done(((bf16[512,128]{1,0:T(8,128)(2,1)}, bf16[512,128]{1,0:T(8,128)(2,1)}), (bf16[512,128]{1,0:T(8,128)(2,1)}, bf16[512,128]{1,0:T(8,128)(2,1)})) %all-reduce.4.cloned.1.call-update) | async-done | bytes 262160 | tf_op jit(solution)/shard_map/psum | solution.py:14
  164.0 350.8 %while.19 = (s32[]{:T(128)}, f32[1,4,512]{2,1,0:T(4,128)S(1)}, f32[1,4,512]{2,1,0:T(4,128)S(1)}, f32[1,4,512,128]{3,2,1,0:T(8,128)S(1)}, bf16[2,256,128]{2,1,0:T...) while((s32[]{:T(128)}, f32[1,4,512]{2,1,0:T(4,128)S(1)}, ...), condition=%wide.region_9.10_spmd, body=%wide.region_6.9_spmd.sunk | while | flops 275781632 | bytes 9962640 | solution.py:85
  177.3 7.0 %collective-permute-done = bf16[2,256,128]{2,1,0:T(8,128)(2,1)S(1)} collective-permute-done((bf16[2,256,128]{2,1,0:T(8,128)(2,1)S(1)}, bf16[2,256,128]{2,1,0:T(8,128)(2,1)S(1)}, u32[]{:S(2)}, u32[]{:S(2)}) %collective-permute-start) | collective-permute-done | bytes 131104 | tf_op jit(solution)/shard_map/while/body/eval_jaxpr/ppermute | solution.py:20
  188.4 7.0 %collective-permute-done = bf16[2,256,128]{2,1,0:T(8,128)(2,1)S(1)} collective-permute-done((bf16[2,256,128]{2,1,0:T(8,128)(2,1)S(1)}, bf16[2,256,128]{2,1,0:T(8,128)(2,1)S(1)}, u32[]{:S(2)}, u32[]{:S(2)}) %collective-permute-start) | collective-permute-done | bytes 131104 | tf_op jit(solution)/shard_map/while/body/eval_jaxpr/ppermute | solution.py:20
  199.5 7.3 %collective-permute-done = bf16[2,256,128]{2,1,0:T(8,128)(2,1)S(1)} collective-permute-done((bf16[2,256,128]{2,1,0:T(8,128)(2,1)S(1)}, bf16[2,256,128]{2,1,0:T(8,128)(2,1)S(1)}, u32[]{:S(2)}, u32[]{:S(2)}) %collective-permute-start) | collective-permute-done | bytes 131104 | tf_op jit(solution)/shard_map/while/body/eval_jaxpr/ppermute | solution.py:20
  210.9 8.4 %collective-permute-done = bf16[2,256,128]{2,1,0:T(8,128)(2,1)S(1)} collective-permute-done((bf16[2,256,128]{2,1,0:T(8,128)(2,1)S(1)}, bf16[2,256,128]{2,1,0:T(8,128)(2,1)S(1)}, u32[]{:S(2)}, u32[]{:S(2)}) %collective-permute-start) | collective-permute-done | bytes 131104 | tf_op jit(solution)/shard_map/while/body/eval_jaxpr/ppermute | solution.py:20
  223.4 7.6 %collective-permute-done = bf16[2,256,128]{2,1,0:T(8,128)(2,1)S(1)} collective-permute-done((bf16[2,256,128]{2,1,0:T(8,128)(2,1)S(1)}, bf16[2,256,128]{2,1,0:T(8,128)(2,1)S(1)}, u32[]{:S(2)}, u32[]{:S(2)}) %collective-permute-start) | collective-permute-done | bytes 131104 | tf_op jit(solution)/shard_map/while/body/eval_jaxpr/ppermute | solution.py:20
  235.1 7.0 %collective-permute-done = bf16[2,256,128]{2,1,0:T(8,128)(2,1)S(1)} collective-permute-done((bf16[2,256,128]{2,1,0:T(8,128)(2,1)S(1)}, bf16[2,256,128]{2,1,0:T(8,128)(2,1)S(1)}, u32[]{:S(2)}, u32[]{:S(2)}) %collective-permute-start) | collective-permute-done | bytes 131104 | tf_op jit(solution)/shard_map/while/body/eval_jaxpr/ppermute | solution.py:20
  246.2 7.0 %collective-permute-done = bf16[2,256,128]{2,1,0:T(8,128)(2,1)S(1)} collective-permute-done((bf16[2,256,128]{2,1,0:T(8,128)(2,1)S(1)}, bf16[2,256,128]{2,1,0:T(8,128)(2,1)S(1)}, u32[]{:S(2)}, u32[]{:S(2)}) %collective-permute-start) | collective-permute-done | bytes 131104 | tf_op jit(solution)/shard_map/while/body/eval_jaxpr/ppermute | solution.py:20
  257.3 7.0 %collective-permute-done = bf16[2,256,128]{2,1,0:T(8,128)(2,1)S(1)} collective-permute-done((bf16[2,256,128]{2,1,0:T(8,128)(2,1)S(1)}, bf16[2,256,128]{2,1,0:T(8,128)(2,1)S(1)}, u32[]{:S(2)}, u32[]{:S(2)}) %collective-permute-start) | collective-permute-done | bytes 131104 | tf_op jit(solution)/shard_map/while/body/eval_jaxpr/ppermute | solution.py:20
  268.5 7.0 %collective-permute-done = bf16[2,256,128]{2,1,0:T(8,128)(2,1)S(1)} collective-permute-done((bf16[2,256,128]{2,1,0:T(8,128)(2,1)S(1)}, bf16[2,256,128]{2,1,0:T(8,128)(2,1)S(1)}, u32[]{:S(2)}, u32[]{:S(2)}) %collective-permute-start) | collective-permute-done | bytes 131104 | tf_op jit(solution)/shard_map/while/body/eval_jaxpr/ppermute | solution.py:20
  279.6 7.0 %collective-permute-done = bf16[2,256,128]{2,1,0:T(8,128)(2,1)S(1)} collective-permute-done((bf16[2,256,128]{2,1,0:T(8,128)(2,1)S(1)}, bf16[2,256,128]{2,1,0:T(8,128)(2,1)S(1)}, u32[]{:S(2)}, u32[]{:S(2)}) %collective-permute-start) | collective-permute-done | bytes 131104 | tf_op jit(solution)/shard_map/while/body/eval_jaxpr/ppermute | solution.py:20
  290.7 7.0 %collective-permute-done = bf16[2,256,128]{2,1,0:T(8,128)(2,1)S(1)} collective-permute-done((bf16[2,256,128]{2,1,0:T(8,128)(2,1)S(1)}, bf16[2,256,128]{2,1,0:T(8,128)(2,1)S(1)}, u32[]{:S(2)}, u32[]{:S(2)}) %collective-permute-start) | collective-permute-done | bytes 131104 | tf_op jit(solution)/shard_map/while/body/eval_jaxpr/ppermute | solution.py:20
  301.9 7.0 %collective-permute-done = bf16[2,256,128]{2,1,0:T(8,128)(2,1)S(1)} collective-permute-done((bf16[2,256,128]{2,1,0:T(8,128)(2,1)S(1)}, bf16[2,256,128]{2,1,0:T(8,128)(2,1)S(1)}, u32[]{:S(2)}, u32[]{:S(2)}) %collective-permute-start) | collective-permute-done | bytes 131104 | tf_op jit(solution)/shard_map/while/body/eval_jaxpr/ppermute | solution.py:20
  313.0 8.2 %collective-permute-done = bf16[2,256,128]{2,1,0:T(8,128)(2,1)S(1)} collective-permute-done((bf16[2,256,128]{2,1,0:T(8,128)(2,1)S(1)}, bf16[2,256,128]{2,1,0:T(8,128)(2,1)S(1)}, u32[]{:S(2)}, u32[]{:S(2)}) %collective-permute-start) | collective-permute-done | bytes 131104 | tf_op jit(solution)/shard_map/while/body/eval_jaxpr/ppermute | solution.py:20
  325.3 7.6 %collective-permute-done = bf16[2,256,128]{2,1,0:T(8,128)(2,1)S(1)} collective-permute-done((bf16[2,256,128]{2,1,0:T(8,128)(2,1)S(1)}, bf16[2,256,128]{2,1,0:T(8,128)(2,1)S(1)}, u32[]{:S(2)}, u32[]{:S(2)}) %collective-permute-start) | collective-permute-done | bytes 131104 | tf_op jit(solution)/shard_map/while/body/eval_jaxpr/ppermute | solution.py:20
  337.0 7.0 %collective-permute-done = bf16[2,256,128]{2,1,0:T(8,128)(2,1)S(1)} collective-permute-done((bf16[2,256,128]{2,1,0:T(8,128)(2,1)S(1)}, bf16[2,256,128]{2,1,0:T(8,128)(2,1)S(1)}, u32[]{:S(2)}, u32[]{:S(2)}) %collective-permute-start) | collective-permute-done | bytes 131104 | tf_op jit(solution)/shard_map/while/body/eval_jaxpr/ppermute | solution.py:20
  348.1 7.0 %collective-permute-done = bf16[2,256,128]{2,1,0:T(8,128)(2,1)S(1)} collective-permute-done((bf16[2,256,128]{2,1,0:T(8,128)(2,1)S(1)}, bf16[2,256,128]{2,1,0:T(8,128)(2,1)S(1)}, u32[]{:S(2)}, u32[]{:S(2)}) %collective-permute-start) | collective-permute-done | bytes 131104 | tf_op jit(solution)/shard_map/while/body/eval_jaxpr/ppermute | solution.py:20
  359.2 7.0 %collective-permute-done = bf16[2,256,128]{2,1,0:T(8,128)(2,1)S(1)} collective-permute-done((bf16[2,256,128]{2,1,0:T(8,128)(2,1)S(1)}, bf16[2,256,128]{2,1,0:T(8,128)(2,1)S(1)}, u32[]{:S(2)}, u32[]{:S(2)}) %collective-permute-start) | collective-permute-done | bytes 131104 | tf_op jit(solution)/shard_map/while/body/eval_jaxpr/ppermute | solution.py:20
  370.4 7.0 %collective-permute-done = bf16[2,256,128]{2,1,0:T(8,128)(2,1)S(1)} collective-permute-done((bf16[2,256,128]{2,1,0:T(8,128)(2,1)S(1)}, bf16[2,256,128]{2,1,0:T(8,128)(2,1)S(1)}, u32[]{:S(2)}, u32[]{:S(2)}) %collective-permute-start) | collective-permute-done | bytes 131104 | tf_op jit(solution)/shard_map/while/body/eval_jaxpr/ppermute | solution.py:20
  414.9 8.2 %collective-permute-done = bf16[2,256,128]{2,1,0:T(8,128)(2,1)S(1)} collective-permute-done((bf16[2,256,128]{2,1,0:T(8,128)(2,1)S(1)}, bf16[2,256,128]{2,1,0:T(8,128)(2,1)S(1)}, u32[]{:S(2)}, u32[]{:S(2)}) %collective-permute-start) | collective-permute-done | bytes 131104 | tf_op jit(solution)/shard_map/while/body/eval_jaxpr/ppermute | solution.py:20
  427.2 7.6 %collective-permute-done = bf16[2,256,128]{2,1,0:T(8,128)(2,1)S(1)} collective-permute-done((bf16[2,256,128]{2,1,0:T(8,128)(2,1)S(1)}, bf16[2,256,128]{2,1,0:T(8,128)(2,1)S(1)}, u32[]{:S(2)}, u32[]{:S(2)}) %collective-permute-start) | collective-permute-done | bytes 131104 | tf_op jit(solution)/shard_map/while/body/eval_jaxpr/ppermute | solution.py:20
  494.5 7.0 %collective-permute-done = bf16[2,256,128]{2,1,0:T(8,128)(2,1)S(1)} collective-permute-done((bf16[2,256,128]{2,1,0:T(8,128)(2,1)S(1)}, bf16[2,256,128]{2,1,0:T(8,128)(2,1)S(1)}, u32[]{:S(2)}, u32[]{:S(2)}) %collective-permute-start) | collective-permute-done | bytes 131104 | tf_op jit(solution)/shard_map/while/body/eval_jaxpr/ppermute | solution.py:20
  521.8 33.5 %reduce-scatter.2.cloned.1.call-done = bf16[512,512]{1,0:T(8,128)(2,1)} async-done(((bf16[512,4096]{1,0:T(8,128)(2,1)}), bf16[512,512]{1,0:T(8,128)(2,1)}) %reduce-scatter.2.cloned.1.call-update) | async-done | bytes 524304 | tf_op jit(solution)/shard_map/reduce_scatter | solution.py:93
  (294 shorter events, 220.0 us)
Async XLA Ops:
  6.5 149.7 %all-reduce.4.cloned.1.call-start = ((), (), s32[]{:S(2)}) async-start(), calls=%async_computation.2 | async-start | bytes 524288 | tf_op jit(solution)/shard_map/psum | solution.py:14
  7.3 548.0 %reduce-scatter.2.cloned.1.call-start = ((), (), s32[]{:S(2)}) async-start(), calls=%async_computation.1 | async-start | bytes 4718592 | tf_op jit(solution)/shard_map/reduce_scatter | solution.py:93
  164.2 9.0 %collective-permute-start = (bf16[2,256,128]{2,1,0:T(8,128)(2,1)S(1)}, bf16[2,256,128]{2,1,0:T(8,128)(2,1)S(1)}, u32[]{:S(2)}, u32[]{:S(2)}) collective-permute-start(bf16[2,256,128]{2,1,0:T(8,128)(2,1)S(1)} %get-tuple-element.234), channel_id=1, source_target_pairs={{0,8},{8,16},{16,24},{24,32},{32,40},{40,48},{48,56},{56,64},{64,7... | collective-permute-start | bytes 393224 | tf_op jit(solution)/shard_map/while/body/eval_jaxpr/ppermute | solution.py:20
  197.6 9.2 %collective-permute-start = (bf16[2,256,128]{2,1,0:T(8,128)(2,1)S(1)}, bf16[2,256,128]{2,1,0:T(8,128)(2,1)S(1)}, u32[]{:S(2)}, u32[]{:S(2)}) collective-permute-start(bf16[2,256,128]{2,1,0:T(8,128)(2,1)S(1)} %get-tuple-element.234), channel_id=1, source_target_pairs={{0,8},{8,16},{16,24},{24,32},{32,40},{40,48},{48,56},{56,64},{64,7... | collective-permute-start | bytes 393224 | tf_op jit(solution)/shard_map/while/body/eval_jaxpr/ppermute | solution.py:20
  209.0 10.3 %collective-permute-start = (bf16[2,256,128]{2,1,0:T(8,128)(2,1)S(1)}, bf16[2,256,128]{2,1,0:T(8,128)(2,1)S(1)}, u32[]{:S(2)}, u32[]{:S(2)}) collective-permute-start(bf16[2,256,128]{2,1,0:T(8,128)(2,1)S(1)} %get-tuple-element.234), channel_id=1, source_target_pairs={{0,8},{8,16},{16,24},{24,32},{32,40},{40,48},{48,56},{56,64},{64,7... | collective-permute-start | bytes 393224 | tf_op jit(solution)/shard_map/while/body/eval_jaxpr/ppermute | solution.py:20
  221.5 9.5 %collective-permute-start = (bf16[2,256,128]{2,1,0:T(8,128)(2,1)S(1)}, bf16[2,256,128]{2,1,0:T(8,128)(2,1)S(1)}, u32[]{:S(2)}, u32[]{:S(2)}) collective-permute-start(bf16[2,256,128]{2,1,0:T(8,128)(2,1)S(1)} %get-tuple-element.234), channel_id=1, source_target_pairs={{0,8},{8,16},{16,24},{24,32},{32,40},{40,48},{48,56},{56,64},{64,7... | collective-permute-start | bytes 393224 | tf_op jit(solution)/shard_map/while/body/eval_jaxpr/ppermute | solution.py:20
  233.1 9.0 %collective-permute-start = (bf16[2,256,128]{2,1,0:T(8,128)(2,1)S(1)}, bf16[2,256,128]{2,1,0:T(8,128)(2,1)S(1)}, u32[]{:S(2)}, u32[]{:S(2)}) collective-permute-start(bf16[2,256,128]{2,1,0:T(8,128)(2,1)S(1)} %get-tuple-element.234), channel_id=1, source_target_pairs={{0,8},{8,16},{16,24},{24,32},{32,40},{40,48},{48,56},{56,64},{64,7... | collective-permute-start | bytes 393224 | tf_op jit(solution)/shard_map/while/body/eval_jaxpr/ppermute | solution.py:20
  244.3 9.0 %collective-permute-start = (bf16[2,256,128]{2,1,0:T(8,128)(2,1)S(1)}, bf16[2,256,128]{2,1,0:T(8,128)(2,1)S(1)}, u32[]{:S(2)}, u32[]{:S(2)}) collective-permute-start(bf16[2,256,128]{2,1,0:T(8,128)(2,1)S(1)} %get-tuple-element.234), channel_id=1, source_target_pairs={{0,8},{8,16},{16,24},{24,32},{32,40},{40,48},{48,56},{56,64},{64,7... | collective-permute-start | bytes 393224 | tf_op jit(solution)/shard_map/while/body/eval_jaxpr/ppermute | solution.py:20
  266.5 9.0 %collective-permute-start = (bf16[2,256,128]{2,1,0:T(8,128)(2,1)S(1)}, bf16[2,256,128]{2,1,0:T(8,128)(2,1)S(1)}, u32[]{:S(2)}, u32[]{:S(2)}) collective-permute-start(bf16[2,256,128]{2,1,0:T(8,128)(2,1)S(1)} %get-tuple-element.234), channel_id=1, source_target_pairs={{0,8},{8,16},{16,24},{24,32},{32,40},{40,48},{48,56},{56,64},{64,7... | collective-permute-start | bytes 393224 | tf_op jit(solution)/shard_map/while/body/eval_jaxpr/ppermute | solution.py:20
  288.8 9.0 %collective-permute-start = (bf16[2,256,128]{2,1,0:T(8,128)(2,1)S(1)}, bf16[2,256,128]{2,1,0:T(8,128)(2,1)S(1)}, u32[]{:S(2)}, u32[]{:S(2)}) collective-permute-start(bf16[2,256,128]{2,1,0:T(8,128)(2,1)S(1)} %get-tuple-element.234), channel_id=1, source_target_pairs={{0,8},{8,16},{16,24},{24,32},{32,40},{40,48},{48,56},{56,64},{64,7... | collective-permute-start | bytes 393224 | tf_op jit(solution)/shard_map/while/body/eval_jaxpr/ppermute | solution.py:20
  299.9 9.0 %collective-permute-start = (bf16[2,256,128]{2,1,0:T(8,128)(2,1)S(1)}, bf16[2,256,128]{2,1,0:T(8,128)(2,1)S(1)}, u32[]{:S(2)}, u32[]{:S(2)}) collective-permute-start(bf16[2,256,128]{2,1,0:T(8,128)(2,1)S(1)} %get-tuple-element.234), channel_id=1, source_target_pairs={{0,8},{8,16},{16,24},{24,32},{32,40},{40,48},{48,56},{56,64},{64,7... | collective-permute-start | bytes 393224 | tf_op jit(solution)/shard_map/while/body/eval_jaxpr/ppermute | solution.py:20
  311.1 10.1 %collective-permute-start = (bf16[2,256,128]{2,1,0:T(8,128)(2,1)S(1)}, bf16[2,256,128]{2,1,0:T(8,128)(2,1)S(1)}, u32[]{:S(2)}, u32[]{:S(2)}) collective-permute-start(bf16[2,256,128]{2,1,0:T(8,128)(2,1)S(1)} %get-tuple-element.234), channel_id=1, source_target_pairs={{0,8},{8,16},{16,24},{24,32},{32,40},{40,48},{48,56},{56,64},{64,7... | collective-permute-start | bytes 393224 | tf_op jit(solution)/shard_map/while/body/eval_jaxpr/ppermute | solution.py:20
  323.4 9.5 %collective-permute-start = (bf16[2,256,128]{2,1,0:T(8,128)(2,1)S(1)}, bf16[2,256,128]{2,1,0:T(8,128)(2,1)S(1)}, u32[]{:S(2)}, u32[]{:S(2)}) collective-permute-start(bf16[2,256,128]{2,1,0:T(8,128)(2,1)S(1)} %get-tuple-element.234), channel_id=1, source_target_pairs={{0,8},{8,16},{16,24},{24,32},{32,40},{40,48},{48,56},{56,64},{64,7... | collective-permute-start | bytes 393224 | tf_op jit(solution)/shard_map/while/body/eval_jaxpr/ppermute | solution.py:20
  335.0 9.0 %collective-permute-start = (bf16[2,256,128]{2,1,0:T(8,128)(2,1)S(1)}, bf16[2,256,128]{2,1,0:T(8,128)(2,1)S(1)}, u32[]{:S(2)}, u32[]{:S(2)}) collective-permute-start(bf16[2,256,128]{2,1,0:T(8,128)(2,1)S(1)} %get-tuple-element.234), channel_id=1, source_target_pairs={{0,8},{8,16},{16,24},{24,32},{32,40},{40,48},{48,56},{56,64},{64,7... | collective-permute-start | bytes 393224 | tf_op jit(solution)/shard_map/while/body/eval_jaxpr/ppermute | solution.py:20
  357.3 9.0 %collective-permute-start = (bf16[2,256,128]{2,1,0:T(8,128)(2,1)S(1)}, bf16[2,256,128]{2,1,0:T(8,128)(2,1)S(1)}, u32[]{:S(2)}, u32[]{:S(2)}) collective-permute-start(bf16[2,256,128]{2,1,0:T(8,128)(2,1)S(1)} %get-tuple-element.234), channel_id=1, source_target_pairs={{0,8},{8,16},{16,24},{24,32},{32,40},{40,48},{48,56},{56,64},{64,7... | collective-permute-start | bytes 393224 | tf_op jit(solution)/shard_map/while/body/eval_jaxpr/ppermute | solution.py:20
  368.4 9.0 %collective-permute-start = (bf16[2,256,128]{2,1,0:T(8,128)(2,1)S(1)}, bf16[2,256,128]{2,1,0:T(8,128)(2,1)S(1)}, u32[]{:S(2)}, u32[]{:S(2)}) collective-permute-start(bf16[2,256,128]{2,1,0:T(8,128)(2,1)S(1)} %get-tuple-element.234), channel_id=1, source_target_pairs={{0,8},{8,16},{16,24},{24,32},{32,40},{40,48},{48,56},{56,64},{64,7... | collective-permute-start | bytes 393224 | tf_op jit(solution)/shard_map/while/body/eval_jaxpr/ppermute | solution.py:20
  390.7 9.0 %collective-permute-start = (bf16[2,256,128]{2,1,0:T(8,128)(2,1)S(1)}, bf16[2,256,128]{2,1,0:T(8,128)(2,1)S(1)}, u32[]{:S(2)}, u32[]{:S(2)}) collective-permute-start(bf16[2,256,128]{2,1,0:T(8,128)(2,1)S(1)} %get-tuple-element.234), channel_id=1, source_target_pairs={{0,8},{8,16},{16,24},{24,32},{32,40},{40,48},{48,56},{56,64},{64,7... | collective-permute-start | bytes 393224 | tf_op jit(solution)/shard_map/while/body/eval_jaxpr/ppermute | solution.py:20
  413.0 10.1 %collective-permute-start = (bf16[2,256,128]{2,1,0:T(8,128)(2,1)S(1)}, bf16[2,256,128]{2,1,0:T(8,128)(2,1)S(1)}, u32[]{:S(2)}, u32[]{:S(2)}) collective-permute-start(bf16[2,256,128]{2,1,0:T(8,128)(2,1)S(1)} %get-tuple-element.234), channel_id=1, source_target_pairs={{0,8},{8,16},{16,24},{24,32},{32,40},{40,48},{48,56},{56,64},{64,7... | collective-permute-start | bytes 393224 | tf_op jit(solution)/shard_map/while/body/eval_jaxpr/ppermute | solution.py:20
  425.2 9.5 %collective-permute-start = (bf16[2,256,128]{2,1,0:T(8,128)(2,1)S(1)}, bf16[2,256,128]{2,1,0:T(8,128)(2,1)S(1)}, u32[]{:S(2)}, u32[]{:S(2)}) collective-permute-start(bf16[2,256,128]{2,1,0:T(8,128)(2,1)S(1)} %get-tuple-element.234), channel_id=1, source_target_pairs={{0,8},{8,16},{16,24},{24,32},{32,40},{40,48},{48,56},{56,64},{64,7... | collective-permute-start | bytes 393224 | tf_op jit(solution)/shard_map/while/body/eval_jaxpr/ppermute | solution.py:20
  436.9 9.0 %collective-permute-start = (bf16[2,256,128]{2,1,0:T(8,128)(2,1)S(1)}, bf16[2,256,128]{2,1,0:T(8,128)(2,1)S(1)}, u32[]{:S(2)}, u32[]{:S(2)}) collective-permute-start(bf16[2,256,128]{2,1,0:T(8,128)(2,1)S(1)} %get-tuple-element.234), channel_id=1, source_target_pairs={{0,8},{8,16},{16,24},{24,32},{32,40},{40,48},{48,56},{56,64},{64,7... | collective-permute-start | bytes 393224 | tf_op jit(solution)/shard_map/while/body/eval_jaxpr/ppermute | solution.py:20
  459.2 9.0 %collective-permute-start = (bf16[2,256,128]{2,1,0:T(8,128)(2,1)S(1)}, bf16[2,256,128]{2,1,0:T(8,128)(2,1)S(1)}, u32[]{:S(2)}, u32[]{:S(2)}) collective-permute-start(bf16[2,256,128]{2,1,0:T(8,128)(2,1)S(1)} %get-tuple-element.234), channel_id=1, source_target_pairs={{0,8},{8,16},{16,24},{24,32},{32,40},{40,48},{48,56},{56,64},{64,7... | collective-permute-start | bytes 393224 | tf_op jit(solution)/shard_map/while/body/eval_jaxpr/ppermute | solution.py:20
  481.5 9.0 %collective-permute-start = (bf16[2,256,128]{2,1,0:T(8,128)(2,1)S(1)}, bf16[2,256,128]{2,1,0:T(8,128)(2,1)S(1)}, u32[]{:S(2)}, u32[]{:S(2)}) collective-permute-start(bf16[2,256,128]{2,1,0:T(8,128)(2,1)S(1)} %get-tuple-element.234), channel_id=1, source_target_pairs={{0,8},{8,16},{16,24},{24,32},{32,40},{40,48},{48,56},{56,64},{64,7... | collective-permute-start | bytes 393224 | tf_op jit(solution)/shard_map/while/body/eval_jaxpr/ppermute | solution.py:20
  492.6 9.0 %collective-permute-start = (bf16[2,256,128]{2,1,0:T(8,128)(2,1)S(1)}, bf16[2,256,128]{2,1,0:T(8,128)(2,1)S(1)}, u32[]{:S(2)}, u32[]{:S(2)}) collective-permute-start(bf16[2,256,128]{2,1,0:T(8,128)(2,1)S(1)} %get-tuple-element.234), channel_id=1, source_target_pairs={{0,8},{8,16},{16,24},{24,32},{32,40},{40,48},{48,56},{56,64},{64,7... | collective-permute-start | bytes 393224 | tf_op jit(solution)/shard_map/while/body/eval_jaxpr/ppermute | solution.py:20
  503.7 9.0 %collective-permute-start = (bf16[2,256,128]{2,1,0:T(8,128)(2,1)S(1)}, bf16[2,256,128]{2,1,0:T(8,128)(2,1)S(1)}, u32[]{:S(2)}, u32[]{:S(2)}) collective-permute-start(bf16[2,256,128]{2,1,0:T(8,128)(2,1)S(1)} %get-tuple-element.234), channel_id=1, source_target_pairs={{0,8},{8,16},{16,24},{24,32},{32,40},{40,48},{48,56},{56,64},{64,7... | collective-permute-start | bytes 393224 | tf_op jit(solution)/shard_map/while/body/eval_jaxpr/ppermute | solution.py:20
  (14 other events, 104.0 us)
Sparse Core Ops, SparseCore 0:
  10.9 145.3 all-reduce.3
  522.0 33.2 reduce-scatter.1
where the time goes:
time: 567 us; the launch traced here: 562 us
  waiting for transfers between devices  394 us (69%)
  matrix products  62.1 us (11%)
  starting transfers between devices  61 us (11%)
  other arithmetic  20.8 us (4%)
  between operations  14.2 us (3%)
  local copies, waits for them, and re-layouts  7.13 us (1%)
    ppermute x31, waiting for transfers between devices, passed_along(): return lax.ppermute(block, axis, route)  222 us
    psum x1, waiting for transfers between devices, from_root(): return lax.psum(jnp.where(mine, shard, jnp.zeros_like(shard)), axis)  139 us
    ppermute x31, starting transfers between devices, passed_along(): return lax.ppermute(block, axis, route)  60.9 us
    dot_general x33, matrix products, absorb(): jnp.einsum('hgqk,khd->hgqd', weights.astype(jnp.bfloat16), val_three, pre...  37 us
    reduce_scatter x1, waiting for transfers between devices, on_device(): lax.psum_scatter(partial_value.astype(jnp.bfloat16), 'head', scatter_dime...  33.5 us
    dot_general x33, matrix products, absorb(): jnp.einsum('qhgd,khd->hgqk', queries4, key_three, preferred_element_type=...  18.6 us
    reduce_sum x33, other arithmetic, absorb(): total = total * factor + jnp.sum(weights, axis=-1)  18.2 us
  transfers between devices with their start and end apart: 33, of which 33 were waited for; matrix products, arithmetic and copies ran while one was open for 2% of the time, Pallas kernels for 0%

commit v1 on v0

v1 whole, which is shorter than its diff:
```python
import jax
import jax.numpy as jnp
from jax import lax
from jax.experimental import pallas as pl
from jax.experimental.pallas import tpu as pltpu
from jax.sharding import PartitionSpec as P

HEAD = 128
LOG2E = 1.4426950408889634
LIMIT = 2.0**100
NEGATIVE = -1e30
NT = (((1,), (1,)), ((), ()))
TN = (((0,), (0,)), ((), ()))


def select_kernel(kept_ref, key_ref, value_ref, out_ref):
    length, keep = key_ref.shape[0], kept_ref.shape[1]
    rows = lax.broadcasted_iota(jnp.int32, (length, keep), 0)
    chosen = jnp.where(rows == kept_ref[...], 1.0, 0.0).astype(jnp.bfloat16)
    for at, ref in enumerate((key_ref, value_ref)):
        out_ref[:, at * HEAD : (at + 1) * HEAD] = lax.dot_general(
            chosen, ref[...], TN, preferred_element_type=jnp.float32
        ).astype(jnp.bfloat16)


def select(kept, keys, values):
    return pl.pallas_call(
        select_kernel,
        out_shape=jax.ShapeDtypeStruct((kept.shape[1], 2 * HEAD), jnp.bfloat16),
        name="select_kept",
    )(kept, keys, values)


def attend_kernel(
    place_ref, q_ref, k_ref, v_ref, anchor_ref, kept_ref, w_ref, out_ref, acc_ref, peak_ref, att_ref
):
    mine, used = place_ref[0], place_ref[1]
    length, heads = q_ref.shape[0], q_ref.shape[1] // HEAD
    keep = kept_ref.shape[1]
    factor = HEAD**-0.5 * LOG2E

    def query(h):
        return q_ref[:, pl.ds(pl.multiple_of(h * HEAD, HEAD), HEAD)]

    def scores(h, keys):
        return lax.dot_general(query(h), keys, NT, preferred_element_type=jnp.float32) * factor

    def widened(values):
        return jnp.concatenate([values, jnp.ones_like(values)], axis=1)

    def wide(column, width):
        return jnp.concatenate([column] * (width // HEAD), axis=1)

    def product(weights, values):
        return jnp.dot(weights, values, preferred_element_type=jnp.float32)

    def causal():
        shape = (length, length)
        return lax.broadcasted_iota(jnp.int32, shape, 1) <= lax.broadcasted_iota(jnp.int32, shape, 0)

    def in_use():
        return lax.broadcasted_iota(jnp.int32, (length, anchor_ref.shape[0]), 1) < used

    def first(h):
        raw = jnp.where(causal(), scores(h, k_ref[...]), NEGATIVE)
        peak = jnp.broadcast_to(jnp.max(raw, axis=1, keepdims=True), (length, HEAD))
        peak_ref[h] = peak
        weights = jnp.exp2(raw - wide(peak, length)).astype(jnp.bfloat16)
        acc_ref[h] = product(weights, widened(v_ref[...]))

    def fixed(h, keys, values, allowed=None):
        raw = scores(h, keys)
        weights = jnp.exp2(raw - wide(peak_ref[h], keys.shape[0]))
        if allowed is not None:
            weights = jnp.where(allowed, weights, 0.0)
        acc_ref[h] += product(weights.astype(jnp.bfloat16), values)

    def moving(h, keys, values, allowed=None):
        raw = scores(h, keys)
        if allowed is not None:
            raw = jnp.where(allowed, raw, NEGATIVE)
        old = peak_ref[h]
        peak = jnp.maximum(old, jnp.max(raw, axis=1, keepdims=True))
        weights = jnp.exp2(raw - wide(peak, keys.shape[0]))
        if allowed is not None:
            weights = jnp.where(allowed, weights, 0.0)
        peak_ref[h] = peak
        acc_ref[h] = acc_ref[h] * wide(jnp.exp2(old - peak), 2 * HEAD) + product(
            weights.astype(jnp.bfloat16), values
        )

    def group(start, blocks):
        both = kept_ref[pl.ds(start, blocks)].reshape(blocks * keep, 2 * HEAD)
        return both[:, :HEAD], widened(both[:, HEAD:])

    for h in range(heads):
        first(h)

    @pl.when(mine > 0)
    def _():
        values = widened(anchor_ref[:, HEAD:])
        for h in range(heads):
            fixed(h, anchor_ref[:, :HEAD], values, in_use())

    @pl.loop(0, mine // 2)
    def _(pair):
        keys, values = group(pair * 2, 2)
        for h in range(heads):
            fixed(h, keys, values)

    @pl.when(mine % 2 == 1)
    def _():
        keys, values = group(mine - 1, 1)
        for h in range(heads):
            fixed(h, keys, values)

    largest = jnp.max(acc_ref[:, :, HEAD:])

    @pl.when(jnp.logical_not(largest < LIMIT))
    def _():
        @pl.loop(0, heads)
        def _(h):
            first(h)

            @pl.when(mine > 0)
            def _():
                moving(h, anchor_ref[:, :HEAD], widened(anchor_ref[:, HEAD:]), in_use())

            @pl.loop(0, mine)
            def _(block):
                moving(h, *group(block, 1))

    for h in range(heads):
        att_ref[:, h * HEAD : (h + 1) * HEAD] = (
            acc_ref[h, :, :HEAD] / acc_ref[h, :, HEAD:]
        ).astype(jnp.bfloat16)

    @pl.loop(0, out_ref.shape[1] // 512)
    def _(tile):
        columns = pl.ds(pl.multiple_of(tile * 512, 512), 512)
        out_ref[:, columns] = product(att_ref[...], w_ref[:, columns]).astype(jnp.bfloat16)


def attend(place, queries, keys, values, anchor, kept, weight):
    length, width = queries.shape
    heads = width // HEAD
    vmem = pl.BlockSpec(memory_space=pltpu.VMEM)
    return pl.pallas_call(
        attend_kernel,
        out_shape=jax.ShapeDtypeStruct((length, weight.shape[1]), jnp.bfloat16),
        in_specs=[pl.BlockSpec(memory_space=pltpu.SMEM)] + [vmem] * 6,
        out_specs=vmem,
        scratch_shapes=[
            pltpu.VMEM((heads, length, 2 * HEAD), jnp.float32),
            pltpu.VMEM((heads, length, HEAD), jnp.float32),
            pltpu.VMEM((length, width), jnp.bfloat16),
        ],
        compiler_params=pltpu.CompilerParams(vmem_limit_bytes=48 * 2**20),
        name="attend",
    )(place, queries, keys, values, anchor, kept, weight)


def from_first(block, axis):
    me, count = lax.axis_index(axis), lax.axis_size(axis)
    block = jnp.where(me == 0, block, jnp.zeros_like(block))
    step = count // 2
    have = [0]
    while step:
        block = block + lax.ppermute(block, axis, [(i, i + step) for i in have])
        have += [i + step for i in have]
        step //= 2
    return block


def on_device(queries, key_rows, value_rows, kept_positions, anchor_length, output_weight):
    mine = lax.axis_index("ctx")
    kept = lax.all_gather(select(kept_positions, key_rows, value_rows), "ctx")
    anchor = from_first(jnp.concatenate([key_rows, value_rows], axis=1), "ctx")
    place = jnp.concatenate([mine.astype(jnp.int32)[None], anchor_length])
    partial_value = attend(place, queries, key_rows, value_rows, anchor, kept, output_weight)
    return lax.psum_scatter(partial_value, "head", scatter_dimension=1, tiled=True)


def solution(mesh):
    placed = (
        P("ctx", "head"),
        P("ctx", "head"),
        P("ctx", "head"),
        P("head", "ctx"),
        P("head"),
        P("head", None),
    )
    return jax.shard_map(
        on_device, mesh=mesh, in_specs=placed, out_specs=P("ctx", "head"), check_vma=False
    )
```

time: 567 us -> 239 us (0.42)
  waiting for transfers between devices: 394 us -> 129 us
  Pallas kernels: 0 us -> 82.2 us
  matrix products: 62.1 us -> 0 us
  starting transfers between devices: 61 us -> 5.93 us
  other arithmetic: 20.8 us -> 1.44 us
    ppermute x31 -> x5, waiting for transfers between devices: 222 us -> 33.5 us  [from_first(): block = block + lax.ppermute(block, axis, [(i, i + step) for i in have])]
    psum x1 -> x0, waiting for transfers between devices: 139 us -> none  [from_root(): return lax.psum(jnp.where(mine, shard, jnp.zeros_like(shard)), axis)]
    pallas_call x0 -> x2, Pallas kernels: none -> 82.2 us  [the longest x1 80.1 us: attend(): pl.pallas_call(attend_kernel, out_shape=jax.ShapeDtypeStruct((length, wei...]
    dot_general x67 -> x0, matrix products: 62.1 us -> none  [the longest x33 37 us: absorb(): jnp.einsum('hgqk,khd->hgqd', weights.astype(jnp.bfloat16), val_three, pre...]
    ppermute x31 -> x5, starting transfers between devices: 60.9 us -> 5.89 us  [from_first(): block = block + lax.ppermute(block, axis, [(i, i + step) for i in have])]
    all_gather x0 -> x1, waiting for transfers between devices: none -> 42.3 us  [on_device(): kept = lax.all_gather(select(kept_positions, key_rows, value_rows), 'ctx')]
    reduce_scatter x1, waiting for transfers between devices: 33.5 us -> 53.6 us  [on_device(): lax.psum_scatter(partial_value, 'head', scatter_dimension=1, tiled=True)]
    reduce_sum x33 -> x0, other arithmetic: 18.2 us -> none  [absorb(): total = total * factor + jnp.sum(weights, axis=-1)]
  transfers between devices with their start and end apart: 33 -> 7, of which waited for: 33 -> 6; matrix products, arithmetic and copies ran while one was open for 2% -> 1% of each run, Pallas kernels for 0% -> 0%
where the time goes in v1:
time: 239 us; the launch traced here: 235 us
  waiting for transfers between devices  129 us (54%)
  Pallas kernels  82.2 us (34%)
  between operations  14.1 us (6%)
  starting transfers between devices  5.93 us (2%)
    pallas_call x1, Pallas kernels, attend(): pl.pallas_call(attend_kernel, out_shape=jax.ShapeDtypeStruct((length, wei...  80.1 us
    reduce_scatter x1, waiting for transfers between devices, on_device(): lax.psum_scatter(partial_value, 'head', scatter_dimension=1, tiled=True)  53.6 us
    all_gather x1, waiting for transfers between devices, on_device(): kept = lax.all_gather(select(kept_positions, key_rows, value_rows), 'ctx')  42.3 us
    ppermute x5, waiting for transfers between devices, from_first(): block = block + lax.ppermute(block, axis, [(i, i + step) for i in have])  33.5 us
    ppermute x5, starting transfers between devices, from_first(): block = block + lax.ppermute(block, axis, [(i, i + step) for i in have])  5.89 us
  transfers between devices with their start and end apart: 7, of which 6 were waited for; matrix products, arithmetic and copies ran while one was open for 1% of the time, Pallas kernels for 0%

profile of v1, /device:TPU:30, one launch (start us, length us, event | category | flops | bytes accessed | tf_op | source)
XLA Modules:
  0.0 235.1 jit_solution(15865898775146227565)
XLA Ops:
  6.5 2.1 select_kept.1
  8.6 0.0 all-gather.3.cloned.1.call-update
  8.6 0.0 reduce-scatter.2.cloned.1.call-start
  8.7 1.0 maximum_select_fusion
  9.7 0.7 collective-permute-start
  10.4 0.1 add.17
  10.5 1.3 collective-permute-start.1
  11.8 17.7 %collective-permute-done.1 = bf16[512,256]{1,0:T(8,128)(2,1)S(1)} collective-permute-done((bf16[512,256]{1,0:T(8,128)(2,1)S(1)}, bf16[512,256]{1,0:T(8,128)(2,1)S(1)}, u32[]{:S(2)}, u32[]{:S(2)}) %collective-permute-start.1) | collective-permute-done | bytes 262176 | tf_op jit(solution)/shard_map/ppermute | solution.py:169
  29.5 0.1 add.18
  29.5 1.3 collective-permute-start.2
  30.8 6.2 %collective-permute-done.2 = bf16[512,256]{1,0:T(8,128)(2,1)S(1)} collective-permute-done((bf16[512,256]{1,0:T(8,128)(2,1)S(1)}, bf16[512,256]{1,0:T(8,128)(2,1)S(1)}, u32[]{:S(2)}, u32[]{:S(2)}) %collective-permute-start.2) | collective-permute-done | bytes 262176 | tf_op jit(solution)/shard_map/ppermute | solution.py:169
  37.0 0.1 add.19
  37.1 1.3 collective-permute-start.3
  38.4 6.3 %collective-permute-done.3 = bf16[512,256]{1,0:T(8,128)(2,1)S(1)} collective-permute-done((bf16[512,256]{1,0:T(8,128)(2,1)S(1)}, bf16[512,256]{1,0:T(8,128)(2,1)S(1)}, u32[]{:S(2)}, u32[]{:S(2)}) %collective-permute-start.3) | collective-permute-done | bytes 262176 | tf_op jit(solution)/shard_map/ppermute | solution.py:169
  44.7 0.1 add.20
  44.8 1.3 collective-permute-start.4
  46.7 0.1 pad_add_fusion.place_ref
  46.8 3.4 %collective-permute-done.4 = bf16[512,256]{1,0:T(8,128)(2,1)S(1)} collective-permute-done((bf16[512,256]{1,0:T(8,128)(2,1)S(1)}, bf16[512,256]{1,0:T(8,128)(2,1)S(1)}, u32[]{:S(2)}, u32[]{:S(2)}) %collective-permute-start.4) | collective-permute-done | bytes 262176 | tf_op jit(solution)/shard_map/ppermute | solution.py:169
  50.2 0.1 add.21.anchor_ref
  50.3 42.3 %all-gather.3.cloned.1.call-done = bf16[8192,256]{1,0:T(8,128)(2,1)} async-done(((bf16[256,256]{1,0:T(8,128)(2,1)}), bf16[8192,256]{1,0:T(8,128)(2,1)}) %all-gather.3.cloned.1.call-update) | async-done | bytes 4194320 | tf_op jit(solution)/shard_map/all_gather | solution.py:177
  92.6 80.1 %attend.1 = bf16[512,4096]{1,0:T(8,128)(2,1)S(1)} custom-call(s32[2]{0:T(128)S(1)} %pad_add_fusion.place_ref, bf16[512,512]{1,0:T(8,128)(2,1)S(1)} %copy-done.3, bf16[512,128]{1,0:T(8,128)(2,1)S(1)} %copy-done.1, bf16[512,128]{1,0:T(8,128)(2,1)S(1)} %copy-done.2, bf16[512,256]{1,0:T(8,128)(2,1)S(1)} %add.21.anchor_ref, bf16[32,256,256]{2,1,0:T(8,128)(2,1)} %bitcast.2, ...), custom_call_target="tpu_custom_call" | custom-call | tf_op jit(solution)/shard_map/attend/pallas_call | solution.py:148
  172.7 1.9 copy-done
  174.7 0.0 reduce-scatter.2.cloned.1.call-update
  174.7 53.6 %reduce-scatter.2.cloned.1.call-done = bf16[512,512]{1,0:T(8,128)(2,1)} async-done(((bf16[512,4096]{1,0:T(8,128)(2,1)}), bf16[512,512]{1,0:T(8,128)(2,1)}) %reduce-scatter.2.cloned.1.call-update) | async-done | bytes 524304 | tf_op jit(solution)/shard_map/reduce_scatter | solution.py:181
  (9 shorter events, 0.0 us)
Async XLA Ops:
  6.5 86.0 %copy-start.2 = (bf16[512,128]{1,0:T(8,128)(2,1)S(1)}, bf16[512,128]{1,0:T(8,128)(2,1)}, u32[]{:S(2)}) copy-start(bf16[512,128]{1,0:T(8,128)(2,1)} %v_ref.1) | copy-start | bytes 393220
  6.5 86.0 %copy-start.1 = (bf16[512,128]{1,0:T(8,128)(2,1)S(1)}, bf16[512,128]{1,0:T(8,128)(2,1)}, u32[]{:S(2)}) copy-start(bf16[512,128]{1,0:T(8,128)(2,1)} %k_ref.1) | copy-start | bytes 393220
  6.5 86.0 %copy-start.3 = (bf16[512,512]{1,0:T(8,128)(2,1)S(1)}, bf16[512,512]{1,0:T(8,128)(2,1)}, u32[]{:S(2)}) copy-start(bf16[512,512]{1,0:T(8,128)(2,1)} %q_ref.1) | copy-start | bytes 1572868
  6.5 86.0 %all-gather.3.cloned.1.call-start = ((), (), s32[]{:S(2)}) async-start(), calls=%async_computation.2 | async-start | bytes 4325376 | tf_op jit(solution)/shard_map/all_gather | solution.py:177
  8.6 219.6 %reduce-scatter.2.cloned.1.call-start = ((), (), s32[]{:S(2)}) async-start(), calls=%async_computation.1 | async-start | bytes 4718592 | tf_op jit(solution)/shard_map/reduce_scatter | solution.py:181
  9.7 0.7 collective-permute-start
  10.5 19.0 %collective-permute-start.1 = (bf16[512,256]{1,0:T(8,128)(2,1)S(1)}, bf16[512,256]{1,0:T(8,128)(2,1)S(1)}, u32[]{:S(2)}, u32[]{:S(2)}) collective-permute-start(bf16[512,256]{1,0:T(8,128)(2,1)S(1)} %add.17), channel_id=1, source_target_pairs={{0,64},{128,192},{1,65},{129,193},{2,66},{130,194},{3,67},{131,195... | collective-permute-start | bytes 786440 | tf_op jit(solution)/shard_map/ppermute | solution.py:169
  29.5 7.5 %collective-permute-start.2 = (bf16[512,256]{1,0:T(8,128)(2,1)S(1)}, bf16[512,256]{1,0:T(8,128)(2,1)S(1)}, u32[]{:S(2)}, u32[]{:S(2)}) collective-permute-start(bf16[512,256]{1,0:T(8,128)(2,1)S(1)} %add.18), channel_id=1, source_target_pairs={{0,32},{128,160},{64,96},{192,224},{1,33},{129,161},{65,97},{193,2... | collective-permute-start | bytes 786440 | tf_op jit(solution)/shard_map/ppermute | solution.py:169
  37.1 7.6 %collective-permute-start.3 = (bf16[512,256]{1,0:T(8,128)(2,1)S(1)}, bf16[512,256]{1,0:T(8,128)(2,1)S(1)}, u32[]{:S(2)}, u32[]{:S(2)}) collective-permute-start(bf16[512,256]{1,0:T(8,128)(2,1)S(1)} %add.19), channel_id=1, source_target_pairs={{0,16},{128,144},{64,80},{192,208},{32,48},{160,176},{96,112},{224... | collective-permute-start | bytes 786440 | tf_op jit(solution)/shard_map/ppermute | solution.py:169
  44.8 5.4 %collective-permute-start.4 = (bf16[512,256]{1,0:T(8,128)(2,1)S(1)}, bf16[512,256]{1,0:T(8,128)(2,1)S(1)}, u32[]{:S(2)}, u32[]{:S(2)}) collective-permute-start(bf16[512,256]{1,0:T(8,128)(2,1)S(1)} %add.20), channel_id=1, source_target_pairs={{0,8},{128,136},{64,72},{192,200},{32,40},{160,168},{96,104},{224,... | collective-permute-start | bytes 786440 | tf_op jit(solution)/shard_map/ppermute | solution.py:169
  172.7 2.0 copy-start
Sparse Core Ops, SparseCore 0:
  10.0 82.5 all-gather.2
  174.8 53.4 reduce-scatter.1

commit v2 on v1

--- a/solution.py
+++ b/solution.py
@@ -32,11 +32,12 @@
 
 
 def attend_kernel(
-    place_ref, q_ref, k_ref, v_ref, anchor_ref, kept_ref, w_ref, out_ref, acc_ref, peak_ref, att_ref
+    place_ref, q_ref, k_ref, v_ref, anchor_ref, *rest
 ):
+    kept_refs, (out_ref, acc_ref, peak_ref) = rest[:4], rest[4:]
     mine, used = place_ref[0], place_ref[1]
     length, heads = q_ref.shape[0], q_ref.shape[1] // HEAD
-    keep = kept_ref.shape[1]
+    count = kept_refs[0].shape[0]
     factor = HEAD**-0.5 * LOG2E
 
     def query(h):
@@ -90,7 +91,11 @@
         )
 
     def group(start, blocks):
-        both = kept_ref[pl.ds(start, blocks)].reshape(blocks * keep, 2 * HEAD)
+        both = []
+        for block in range(blocks):
+            for ref, at in zip(kept_refs, ring_places(start + block, count)):
+                both.append(ref[at])
+        both = jnp.concatenate(both, axis=0)
         return both[:, :HEAD], widened(both[:, HEAD:])
 
     for h in range(heads):
@@ -131,33 +136,60 @@
                 moving(h, *group(block, 1))
 
     for h in range(heads):
-        att_ref[:, h * HEAD : (h + 1) * HEAD] = (
+        out_ref[:, h * HEAD : (h + 1) * HEAD] = (
             acc_ref[h, :, :HEAD] / acc_ref[h, :, HEAD:]
         ).astype(jnp.bfloat16)
 
-    @pl.loop(0, out_ref.shape[1] // 512)
-    def _(tile):
-        columns = pl.ds(pl.multiple_of(tile * 512, 512), 512)
-        out_ref[:, columns] = product(att_ref[...], w_ref[:, columns]).astype(jnp.bfloat16)
-
-
-def attend(place, queries, keys, values, anchor, kept, weight):
+
+def attend(place, queries, keys, values, anchor, kept):
     length, width = queries.shape
     heads = width // HEAD
     vmem = pl.BlockSpec(memory_space=pltpu.VMEM)
     return pl.pallas_call(
         attend_kernel,
-        out_shape=jax.ShapeDtypeStruct((length, weight.shape[1]), jnp.bfloat16),
-        in_specs=[pl.BlockSpec(memory_space=pltpu.SMEM)] + [vmem] * 6,
+        out_shape=jax.ShapeDtypeStruct((length, width), jnp.bfloat16),
+        in_specs=[pl.BlockSpec(memory_space=pltpu.SMEM)] + [vmem] * 8,
         out_specs=vmem,
         scratch_shapes=[
             pltpu.VMEM((heads, length, 2 * HEAD), jnp.float32),
             pltpu.VMEM((heads, length, HEAD), jnp.float32),
-            pltpu.VMEM((length, width), jnp.bfloat16),
         ],
         compiler_params=pltpu.CompilerParams(vmem_limit_bytes=48 * 2**20),
         name="attend",
-    )(place, queries, keys, values, anchor, kept, weight)
+    )(place, queries, keys, values, anchor, *kept)
+
+
+def project_kernel(place_ref, own_ref, other_ref, own_w_ref, other_w_ref, out_ref):
+    chips = out_ref.shape[0]
+    for step in range(chips):
+        at = lax.rem(place_ref[0] + step, chips)
+        total = jnp.dot(own_ref[...], own_w_ref[at], preferred_element_type=jnp.float32)
+        total += jnp.dot(other_ref[...], other_w_ref[at], preferred_element_type=jnp.float32)
+        out_ref[step] = total.astype(jnp.bfloat16)
+
+
+def project(place, own, other, own_w, other_w):
+    chips, _, columns = own_w.shape
+    vmem = pl.BlockSpec(memory_space=pltpu.VMEM)
+    return pl.pallas_call(
+        project_kernel,
+        out_shape=jax.ShapeDtypeStruct((chips, own.shape[0], columns), jnp.bfloat16),
+        in_specs=[pl.BlockSpec(memory_space=pltpu.SMEM)] + [vmem] * 4,
+        out_specs=vmem,
+        compiler_params=pltpu.CompilerParams(vmem_limit_bytes=48 * 2**20),
+        name="project",
+    )(place, own, other, own_w, other_w)
+
+
+def ring_orders(count):
+    across = [y * 8 + z for z in range(8) for y in range(count // 8)]
+    along = list(range(count))
+    return along, along[::-1], across, across[::-1]
+
+
+def ring_places(block, count):
+    across = block % 8 * (count // 8) + block // 8
+    return block, count - 1 - block, across, count - 1 - across
 
 
 def from_first(block, axis):
@@ -172,13 +204,44 @@
     return block
 
 
+def added(*terms):
+    return sum(term.astype(jnp.float32) for term in terms).astype(jnp.bfloat16)
+
+
 def on_device(queries, key_rows, value_rows, kept_positions, anchor_length, output_weight):
-    mine = lax.axis_index("ctx")
-    kept = lax.all_gather(select(kept_positions, key_rows, value_rows), "ctx")
+    mine, head = lax.axis_index("ctx"), lax.axis_index("head")
+    length, devices = queries.shape[0], lax.axis_size("head")
+    chips, chip, core = devices // 2, head // 2, head % 2
+    swap = [(i, i ^ 1) for i in range(devices)]
+    up = [(i, (i + 2) % devices) for i in range(devices)]
+    down = [(i, (i - 2) % devices) for i in range(devices)]
+
+    retained = select(kept_positions, key_rows, value_rows)
+    orders = ring_orders(lax.axis_size("ctx"))
+    rows = retained.shape[0] // len(orders)
+    kept = [
+        lax.all_gather(retained[at * rows : (at + 1) * rows], "ctx", axis_index_groups=[order])
+        for at, order in enumerate(orders)
+    ]
     anchor = from_first(jnp.concatenate([key_rows, value_rows], axis=1), "ctx")
+
+    weight = output_weight.reshape(output_weight.shape[0], chips, 2, -1).transpose(2, 1, 0, 3)
+    own_w = lax.dynamic_index_in_dim(weight, core, 0, keepdims=False)
+    other_w = lax.ppermute(lax.dynamic_index_in_dim(weight, 1 - core, 0, keepdims=False), "head", swap)
+
     place = jnp.concatenate([mine.astype(jnp.int32)[None], anchor_length])
-    partial_value = attend(place, queries, key_rows, value_rows, anchor, kept, output_weight)
-    return lax.psum_scatter(partial_value, "head", scatter_dimension=1, tiled=True)
+    own = attend(place, queries, key_rows, value_rows, anchor, kept)
+    other = lax.ppermute(own, "head", swap)
+    parts = project(chip.astype(jnp.int32)[None], own, other, own_w, other_w)
+
+    half = length // 2
+    from_below = lax.ppermute(parts[2, :half], "head", up)
+    from_above = lax.ppermute(parts[2, half:], "head", down)
+    upward = jnp.concatenate([added(parts[1, :half], from_below), parts[1, half:]])
+    downward = jnp.concatenate([parts[3, :half], added(parts[3, half:], from_above)])
+    return added(
+        parts[0], lax.ppermute(upward, "head", up), lax.ppermute(downward, "head", down)
+    )
 
 
 def solution(mesh):

time: 239 us -> 583 us (2.44)
  the two profiles are of different devices: /device:TPU:30 before, /device:TPU:254 now
where the time goes in v2:
time: 583 us; the launch traced here: 582 us
  waiting for transfers between devices  436 us (75%)
  Pallas kernels  99.4 us (17%)
  local copies, waits for them, and re-layouts  22.1 us (4%)
  between operations  14 us (2%)
  starting transfers between devices  8.81 us (2%)
    all_gather x4, waiting for transfers between devices, on_device(): lax.all_gather(retained[at * rows:(at + 1) * rows], 'ctx', axis_index_gro...  375 us
    pallas_call x1, Pallas kernels, attend(): pl.pallas_call(attend_kernel, out_shape=jax.ShapeDtypeStruct((length, wid...  93.5 us
    ppermute x5, waiting for transfers between devices, from_first(): block = block + lax.ppermute(block, axis, [(i, i + step) for i in have])  38.2 us
    unnamed x17, local copies, waits for them, and re-layouts  16.5 us
  transfers between devices with their start and end apart: 15, of which 9 were waited for; matrix products, arithmetic and copies ran while one was open for 3% of the time, Pallas kernels for 16%

profile of v2, /device:TPU:254, one launch (start us, length us, event | category | flops | bytes accessed | tf_op | source)
XLA Modules:
  0.0 582.2 jit_solution(17643024062462056719)
XLA Ops:
  6.5 2.0 select_kept.1
  8.5 1.5 fusion.4
  12.1 6.5 %copy.7 = bf16[512,4096]{0,1:T(8,128)(2,1)} copy(bf16[512,4096]{1,0:T(8,128)(2,1)} %param.11) | data formatting | bytes 8388608 | tf_op args[5]
  18.6 4.0 constant_dynamic-slice_fusion
  22.6 2.4 copy.11
  28.2 1.3 collective-permute-start.4
  30.3 38.2 %collective-permute-done.4 = bf16[512,256]{1,0:T(8,128)(2,1)S(1)} collective-permute-done((bf16[512,256]{1,0:T(8,128)(2,1)S(1)}, bf16[512,256]{1,0:T(8,128)(2,1)S(1)}, u32[]{:S(2)}, u32[]{:S(2)}) %collective-permute-start.4) | collective-permute-done | bytes 262176 | tf_op jit(solution)/shard_map/ppermute | solution.py:201
  68.6 15.4 %all-gather.9.cloned.1.call-done = bf16[2048,256]{1,0:T(8,128)(2,1)} async-done(((bf16[64,256]{1,0:T(8,128)(2,1)}), bf16[2048,256]{1,0:T(8,128)(2,1)}) %all-gather.9.cloned.1.call-update) | async-done | bytes 1048592 | tf_op jit(solution)/shard_map/all_gather | solution.py:223
  84.0 142.6 %all-gather.11.cloned.1.call-done = bf16[2048,256]{1,0:T(8,128)(2,1)} async-done(((bf16[64,256]{1,0:T(8,128)(2,1)}), bf16[2048,256]{1,0:T(8,128)(2,1)}) %all-gather.11.cloned.1.call-update) | async-done | bytes 1048592 | tf_op jit(solution)/shard_map/all_gather | solution.py:223
  226.6 74.6 %all-gather.13.cloned.1.call-done = bf16[2048,256]{1,0:T(8,128)(2,1)} async-done(((bf16[64,256]{1,0:T(8,128)(2,1)}), bf16[2048,256]{1,0:T(8,128)(2,1)}) %all-gather.13.cloned.1.call-update) | async-done | bytes 1048592 | tf_op jit(solution)/shard_map/all_gather | solution.py:223
  301.2 142.6 %all-gather.15.cloned.1.call-done = bf16[2048,256]{1,0:T(8,128)(2,1)} async-done(((bf16[64,256]{1,0:T(8,128)(2,1)}), bf16[2048,256]{1,0:T(8,128)(2,1)}) %all-gather.15.cloned.1.call-update) | async-done | bytes 1048592 | tf_op jit(solution)/shard_map/all_gather | solution.py:223
  443.8 1.2 copy-done.2
  445.1 1.2 copy-done.3
  446.3 1.2 copy-done.4
  447.5 1.2 copy-done.5
  448.7 93.5 %attend.1.own_ref = bf16[512,512]{1,0:T(8,128)(2,1)S(1)} custom-call(s32[2]{0:T(128)S(1)} %pad_add_fusion.place_ref, bf16[512,512]{1,0:T(8,128)(2,1)S(1)} %copy-done.6, bf16[512,128]{1,0:T(8,128)(2,1)S(1)} %copy-done, bf16[512,128]{1,0:T(8,128)(2,1)S(1)} %copy-done.1, bf16[512,256]{1,0:T(8,128)(2,1)S(1)} %add.44.anchor_ref, ...), custom_call_target="tpu_custom_call" | custom-call | tf_op jit(solution)/shard_map/attend/pallas_call | solution.py:148
  542.5 2.8 copy.10
  545.3 3.9 project.1
  550.0 1.5 collective-permute-start.9
  551.4 6.7 %collective-permute-done.7 = bf16[256,512]{1,0:T(8,128)(2,1)S(1)} collective-permute-done((bf16[256,512]{1,0:T(8,128)(2,1)S(1)}, bf16[256,512]{1,0:T(8,128)(2,1)S(1)}, u32[]{:S(2)}, u32[]{:S(2)}) %collective-permute-start.7) | collective-permute-done | bytes 262176 | tf_op jit(solution)/shard_map/ppermute | solution.py:238
  558.1 1.5 collective-permute-done.9
  560.2 1.8 collective-permute-start.10
  562.0 11.1 %collective-permute-done.8 = bf16[512,512]{1,0:T(8,128)(2,1)S(1)} collective-permute-done((bf16[512,512]{1,0:T(8,128)(2,1)S(1)}, bf16[512,512]{1,0:T(8,128)(2,1)S(1)}, u32[]{:S(2)}, u32[]{:S(2)}) %collective-permute-start.8) | collective-permute-done | bytes 524320 | tf_op jit(solution)/shard_map/ppermute | solution.py:243
  573.1 1.7 collective-permute-done.10
  (44 shorter events, 7.9 us)
Async XLA Ops:
  6.5 77.4 %all-gather.9.cloned.1.call-start = ((), (), s32[]{:S(2)}) async-start(), calls=%async_computation | async-start | bytes 1081344 | tf_op jit(solution)/shard_map/all_gather | solution.py:223
  10.0 216.6 %all-gather.11.cloned.1.call-start = ((), (), s32[]{:S(2)}) async-start(), calls=%async_computation.1 | async-start | bytes 1081344 | tf_op jit(solution)/shard_map/all_gather | solution.py:223
  10.8 290.4 %all-gather.13.cloned.1.call-start = ((), (), s32[]{:S(2)}) async-start(), calls=%async_computation.2 | async-start | bytes 1081344 | tf_op jit(solution)/shard_map/all_gather | solution.py:223
  11.5 432.3 %all-gather.15.cloned.1.call-start = ((), (), s32[]{:S(2)}) async-start(), calls=%async_computation.3 | async-start | bytes 1081344 | tf_op jit(solution)/shard_map/all_gather | solution.py:223
  22.6 2.4 copy-start
  22.6 2.4 copy-start.1
  25.0 520.4 %collective-permute-start.6 = (bf16[4,512,512]{2,1,0:T(8,128)(2,1)}, bf16[4,512,512]{2,1,0:T(8,128)(2,1)}, u32[]{:S(2)}, u32[]{:S(2)}) collective-permute-start(bf16[4,512,512]{2,1,0:T(8,128)(2,1)} %bitcast.42), channel_id=1, source_target_pairs={{0,1},{1,0},{2,3},{3,2},{4,5},{5,4},{6,7},{7,6},{8,9},{9,8},{10,11... | collective-permute-start | bytes 6291464 | tf_op jit(solution)/shard_map/ppermute | solution.py:230
  25.0 418.8 %copy-start.6 = (bf16[512,512]{1,0:T(8,128)(2,1)S(1)}, bf16[512,512]{1,0:T(8,128)(2,1)}, u32[]{:S(2)}) copy-start(bf16[512,512]{1,0:T(8,128)(2,1)} %q_ref.1) | copy-start | bytes 1572868
  25.0 0.8 collective-permute-start
  25.9 0.7 collective-permute-start.1
  26.7 0.7 collective-permute-start.2
  27.5 0.7 collective-permute-start.3
  28.2 40.2 %collective-permute-start.4 = (bf16[512,256]{1,0:T(8,128)(2,1)S(1)}, bf16[512,256]{1,0:T(8,128)(2,1)S(1)}, u32[]{:S(2)}, u32[]{:S(2)}) collective-permute-start(bf16[512,256]{1,0:T(8,128)(2,1)S(1)} %add.43), channel_id=1, source_target_pairs={{0,8},{128,136},{64,72},{192,200},{32,40},{160,168},{96,104},{224,... | collective-permute-start | bytes 786440 | tf_op jit(solution)/shard_map/ppermute | solution.py:201
  443.8 1.2 copy-start.2
  445.1 1.2 copy-start.3
  446.3 1.2 copy-start.4
  447.5 1.2 copy-start.5
  542.2 3.1 collective-permute-start.5
  549.3 8.8 %collective-permute-start.7 = (bf16[256,512]{1,0:T(8,128)(2,1)S(1)}, bf16[256,512]{1,0:T(8,128)(2,1)S(1)}, u32[]{:S(2)}, u32[]{:S(2)}) collective-permute-start(bf16[256,512]{1,0:T(8,128)(2,1)S(1)} %get-tuple-element.9), channel_id=1, source_target_pairs={{0,2},{1,3},{2,4},{3,5},{4,6},{5,7},{6,0},{7,1},{8,10},{9,11},{10,... | collective-permute-start | bytes 786440 | tf_op jit(solution)/shard_map/ppermute | solution.py:238
  550.0 9.6 %collective-permute-start.9 = (bf16[256,512]{1,0:T(8,128)(2,1)S(1)}, bf16[256,512]{1,0:T(8,128)(2,1)S(1)}, u32[]{:S(2)}, u32[]{:S(2)}) collective-permute-start(bf16[256,512]{1,0:T(8,128)(2,1)S(1)} %get-tuple-element.10), channel_id=1, source_target_pairs={{0,6},{1,7},{2,0},{3,1},{4,2},{5,3},{6,4},{7,5},{8,14},{9,15},{10,... | collective-permute-start | bytes 786440 | tf_op jit(solution)/shard_map/ppermute | solution.py:239
  559.8 13.3 %collective-permute-start.8 = (bf16[512,512]{1,0:T(8,128)(2,1)S(1)}, bf16[512,512]{1,0:T(8,128)(2,1)S(1)}, u32[]{:S(2)}, u32[]{:S(2)}) collective-permute-start(bf16[512,512]{1,0:T(8,128)(2,1)S(1)} %pad_maximum_fusion), channel_id=1, source_target_pairs={{0,2},{1,3},{2,4},{3,5},{4,6},{5,7},{6,0},{7,1},{8,10},{9,11},{10,... | collective-permute-start | bytes 1572872 | tf_op jit(solution)/shard_map/ppermute | solution.py:243
  560.2 14.5 %collective-permute-start.10 = (bf16[512,512]{1,0:T(8,128)(2,1)S(1)}, bf16[512,512]{1,0:T(8,128)(2,1)S(1)}, u32[]{:S(2)}, u32[]{:S(2)}) collective-permute-start(bf16[512,512]{1,0:T(8,128)(2,1)S(1)} %pad_maximum_fusion.1), channel_id=1, source_target_pairs={{0,6},{1,7},{2,0},{3,1},{4,2},{5,3},{6,4},{7,5},{8,14},{9,15},{10,... | collective-permute-start | bytes 1572872 | tf_op jit(solution)/shard_map/ppermute | solution.py:243
Sparse Core Ops, SparseCore 0:
  10.1 73.7 all-gather.8
  85.7 140.8 all-gather.10
  229.2 71.9 all-gather.12
  302.8 140.9 all-gather.14
